TPU v7x, 128 devices: a whole 4x4x4 slice. The times are simulated.
128 devices in a mesh: blk: 8 (over y_lo, x), vslab: 16 (over z, y_hi, core).
Axes of the slice: x: 4, y: 4 (y_hi: 2, y_lo: 2; y = y_hi * 2 + y_lo), z: 4, core: 2. Of those that a mesh axis runs over, the one named last changes fastest.
Arguments:
- amplitudes: float32 [1024, 128, 800], P('blk', 'vslab'), may hold values from -6 to 6
- integrals: float32 [128, 800, 4096], P('vslab', None, 'blk'), may hold values from -0.01953125 to 0.01953125
- ab_energy: float32 [4096], P('blk'), may hold values from 1 to 4
- ij_energy: float32 [1024], replicated, may hold values from -4 to -1
- block_size: int32 [32], replicated, may hold values from 1 to 95, as said below
- block_owner: int32 [32], replicated, may hold values from 0 to 15, as said below
Outputs:
- amplitude_new: float32 [1024, 12288], P(None, ('blk', 'vslab'))
Inputs may be any that keep to these rules, and one draw needn't show every extreme that they name: `block_size`: the blocks of one group fill its 512 pairs exactly; every owner holds at most 96 pairs, and one owner exactly 96. `block_owner`: every owner has two blocks.
All inputs are finite; a program needn't handle non-finite values.
Results may differ from a plain program's by a relative error of at most 0.00007.
Values sent between devices are 32-bit elements; how exact they have to be, the bound alone decides.
No kernel may reach another device: no remote copies, remote signals or barrier semaphores. Data moves between devices by JAX's collectives and lax.ppermute only.
A program may use at most 128 MiB of HBM per device.

v0:
```python
import jax
import jax.numpy as jnp
from jax import lax
from jax.sharding import PartitionSpec as P


def slot_tables(block_size, block_owner, rows, owners, cap):
    count = block_size.shape[0]
    order = jnp.arange(count, dtype=jnp.int32)
    starts = jnp.cumsum(block_size) - block_size
    same = block_owner[:, None] == block_owner[None, :]
    earlier = order[None, :] < order[:, None]
    before = jnp.sum(jnp.where(same & earlier, block_size[None, :], 0), axis=1)
    owner_hot = block_owner[:, None] == jnp.arange(owners, dtype=jnp.int32)[None, :]
    load = jnp.sum(jnp.where(owner_hot, block_size[:, None], 0), axis=0)
    owner_start = jnp.cumsum(load) - load
    block_base = jnp.sum(jnp.where(owner_hot, owner_start[None, :], 0), axis=1)
    shift_by = block_base + before - starts
    row_ids = jnp.arange(rows, dtype=jnp.int32)
    inside = (row_ids[:, None] >= starts[None, :]) & (
        row_ids[:, None] < (starts + block_size)[None, :]
    )
    position = jnp.sum(jnp.where(inside, shift_by[None, :], 0), axis=1) + row_ids
    perm = jnp.zeros((rows,), jnp.int32).at[position].set(row_ids)
    slot_ids = jnp.arange(cap, dtype=jnp.int32)
    valid = slot_ids[None, :] < load[:, None]
    index = jnp.minimum(owner_start[:, None] + slot_ids[None, :], rows - 1)
    source = perm[index]
    return (perm, owner_start, load, source, valid)


def on_device(amplitudes, integrals, ab_energy, ij_energy, block_size, block_owner):
    owners = lax.axis_size("vslab")
    rows = integrals.shape[2]
    cap = 3 * rows // owners
    v_matrix = integrals.reshape(-1, rows)
    t_tile = amplitudes.reshape(amplitudes.shape[0], -1)
    ladder = jnp.dot(
        lax.all_gather(t_tile, "blk", axis=0, tiled=True),
        v_matrix,
        precision=lax.Precision.HIGHEST,
        preferred_element_type=jnp.float32,
    )
    perm, owner_start, load, source, valid = slot_tables(block_size, block_owner, rows, owners, cap)
    mine = lax.axis_index("vslab")
    my_source = lax.dynamic_index_in_dim(source, mine, 0, keepdims=False)
    my_valid = lax.dynamic_index_in_dim(valid, mine, 0, keepdims=False)
    packed = jnp.take(ladder, source.reshape(-1), axis=1)
    packed = jnp.where(valid.reshape(1, -1), packed, 0.0).reshape(ladder.shape[0], owners, cap)
    received = lax.all_to_all(packed, "vslab", split_axis=1, concat_axis=1, tiled=True)
    summed = jnp.sum(received, axis=1)
    denom = jnp.take(ab_energy, my_source)[None, :] - ij_energy[:, None]
    return jnp.where(my_valid[None, :], summed / denom, 0.0)


def solution(mesh):
    placed = (P("blk", "vslab", None), P("vslab", None, "blk"), P("blk"), P(), P(), P())
    return jax.shard_map(
        on_device, mesh=mesh, in_specs=placed, out_specs=P(None, ("blk", "vslab")), check_vma=False
    )
```

profile of v0, /device:TPU:1, one launch (start us, length us, event | category | flops | bytes accessed | tf_op | source)
XLA Modules:
  0.0 425.9 jit_solution(8877421864067574619)
XLA Ops:
  6.5 0.7 all-gather.2.cloned.1.call-update
  7.3 0.8 select_reduce_fusion.3
  8.0 0.1 copy.14
  8.2 0.1 reduce.1
  8.3 0.7 copy.13
  9.1 0.1 reduce
  9.2 0.1 compare_select_fusion.2
  9.3 0.1 reshape.231
  9.4 0.7 select_reduce_fusion.2
  10.1 0.9 select_reduce_fusion.1
  11.0 0.7 add_subtract_fusion
  11.7 0.1 select_reduce_fusion
  11.8 2.4 scatter_custom_fusion
  14.3 9.5 %gather_fusion = s32[1536]{0:T(1024)S(1)} fusion(s32[512]{0:T(512)S(1)} %scatter_custom_fusion, s32[2048]{0:T(1024)S(1)} %pad_clamp_fusion.1), kind=kCustom, calls=%fused_computation | custom fusion | bytes 18432 | tf_op jit(solution)/shard_map/gather | solution.py:28
  23.8 0.1 iota_compare_fusion.4
  23.9 250.5 %all-gather.2.cloned.1.call-done = f32[1024,6400]{0,1:T(8,128)} async-done(((f32[128,6400]{0,1:T(8,128)}), f32[1024,6400]{0,1:T(8,128)}) %all-gather.2.cloned.1.call-update) | async-done | bytes 26214416 | tf_op jit(solution)/shard_map/all_gather | solution.py:39
  274.4 45.6 %fusion.7 = f32[1024,512]{0,1:T(8,128)S(1)} fusion(f32[1024,6400]{0,1:T(8,128)} %all-gather.2.cloned.1.call-done, f32[6400,512]{1,0:T(8,128)} %bitcast.31), kind=kOutput, calls=%fused_computation.36 | convolution fusion | flops 40265318400 | bytes 41418752 | tf_op jit(solution)/shard_map/dot_general | solution.py:38
  320.0 5.8 %gather_fusion.1 = f32[1536,1024]{1,0:T(8,128)} fusion(f32[1024,512]{0,1:T(8,128)S(1)} %fusion.7, s32[2048]{0:T(1024)S(1)} %pad_clamp_fusion), kind=kCustom, calls=%fused_computation.1 | custom fusion | bytes 12589056 | tf_op jit(solution)/shard_map/jit(_take)/gather | solution.py:48
  325.8 4.9 %select_select_fusion = f32[1024,16,96]{0,2,1:T(8,128)} fusion(f32[1024,16,96]{0,2,1:T(8,128)} %bitcast.25, pred[16,96]{1,0:T(8,128)(4,1)S(1)} %get-tuple-element.8, pred[16,96]{1,0:T(8,128)(4,1)S(1)} %get-tuple-element.7), kind=kLoop, calls=%fused_computation.4 | loop fusion | flops 3145728 | bytes 12585984 | tf_op jit(solution)/shard_map/jit(_where)/select_n | solution.py:49
  330.8 10.5 %all-to-all-start = ((f32[1024,16,96]{0,2,1:T(8,128)}), f32[1024,16,96]{0,2,1:T(8,128)}, u32[]{:S(2)}, u32[]{:S(2)}) async-start(f32[1024,16,96]{0,2,1:T(8,128)} %select_select_fusion), calls=%async_computation | async-start | bytes 12582912 | tf_op jit(solution)/shard_map/all_to_all | solution.py:50
  341.3 1.3 gather_fusion.2
  342.6 72.2 %all-to-all-done = f32[1024,16,96]{0,2,1:T(8,128)} async-done(((f32[1024,16,96]{0,2,1:T(8,128)}), f32[1024,16,96]{0,2,1:T(8,128)}, u32[]{:S(2)}, u32[]{:S(2)}) %all-to-all-start) | async-done | bytes 6291488 | tf_op jit(solution)/shard_map/all_to_all | solution.py:50
  414.8 3.4 reduce_sum.52
  418.2 0.9 divide_select_fusion
  (18 shorter events, 0.3 us)
Async XLA Ops:
  6.5 334.7 %copy-start = (f32[512]{0:T(512)S(1)}, f32[512]{0:T(512)}, u32[]{:S(2)}) copy-start(f32[512]{0:T(512)} %param.8) | copy-start | bytes 6148
  6.5 267.8 %all-gather.2.cloned.1.call-start = ((), (), s32[]{:S(2)}) async-start(), calls=%async_computation.1 | async-start | bytes 29491200 | tf_op jit(solution)/shard_map/all_gather | solution.py:39
  330.8 84.0 %all-to-all-start = ((f32[1024,16,96]{0,2,1:T(8,128)}), f32[1024,16,96]{0,2,1:T(8,128)}, u32[]{:S(2)}, u32[]{:S(2)}) async-start(f32[1024,16,96]{0,2,1:T(8,128)} %select_select_fusion), calls=%async_computation | async-start | bytes 12582912 | tf_op jit(solution)/shard_map/all_to_all | solution.py:50
  341.2 76.9 %copy-start.1 = (f32[1024]{0:T(1024)S(1)}, f32[1024]{0:T(1024)}, u32[]{:S(2)}) copy-start(f32[1024]{0:T(1024)} %param.9) | copy-start | bytes 12292
Sparse Core Ops, SparseCore 0:
  8.9 265.4 all-gather.1
where the time goes:
time: 426 us
  waiting for transfers between devices  323 us (76%)
  matrix products  45.6 us (11%)
  local copies, waits for them, and re-layouts  20 us (5%)
  between operations  13.5 us (3%)
  other arithmetic  13 us (3%)
  starting transfers between devices  10.5 us (2%)
    all_gather x1, waiting for transfers between devices, on_device(): lax.all_gather(t_tile, 'blk', axis=0, tiled=True)  250 us
    all_to_all x1, waiting for transfers between devices, on_device(): lax.all_to_all(packed, 'vslab', split_axis=1, concat_axis=1, tiled=True)  72.2 us
    dot_general x1, matrix products, on_device(): jnp.dot(lax.all_gather(t_tile, 'blk', axis=0, tiled=True), v_matrix, prec...  45.6 us
    all_to_all x1, starting transfers between devices, on_device(): lax.all_to_all(packed, 'vslab', split_axis=1, concat_axis=1, tiled=True)  10.5 us
    gather x2, local copies, waits for them, and re-layouts, slot_tables(): source = perm[index]  9.54 us
  transfers between devices with their start and end apart: 2, of which 2 were waited for; matrix products, arithmetic and copies ran while one was open for 4% of the time, Pallas kernels for 0%

commit v1 on v0

--- a/solution.py
+++ b/solution.py
@@ -36,7 +36,9 @@
     v_matrix = integrals.reshape(-1, rows)
     t_tile = amplitudes.reshape(amplitudes.shape[0], -1)
     ladder = jnp.dot(
-        lax.all_gather(t_tile, "blk", axis=0, tiled=True),
+        jnp.concatenate(
+            lax.all_to_all(jnp.stack([t_tile] * lax.axis_size("blk")), "blk", 0, 0), axis=0
+        ),
         v_matrix,
         precision=lax.Precision.HIGHEST,
         preferred_element_type=jnp.float32,

time: 426 us -> 557 us (1.31)
  the two profiles are of different devices: /device:TPU:1 before, /device:TPU:6 now
where the time goes in v1:
time: 557 us; the launch traced here: 556 us
  waiting for transfers between devices  451 us (81%)
  matrix products  45.8 us (8%)
  local copies, waits for them, and re-layouts  33.8 us (6%)
  starting transfers between devices  15.2 us (3%)
  other arithmetic  10.2 us (2%)
    all_to_all x1, waiting for transfers between devices, on_device(): lax.all_to_all(jnp.stack([t_tile] * lax.axis_size('blk')), 'blk', 0, 0)  378 us
    all_to_all x1, waiting for transfers between devices, on_device(): lax.all_to_all(packed, 'vslab', split_axis=1, concat_axis=1, tiled=True)  73 us
    dot_general x1, matrix products, on_device(): jnp.dot(jnp.concatenate(lax.all_to_all(jnp.stack([t_tile] * lax.axis_size...  45.8 us
    another operation x2, local copies, waits for them, and re-layouts, on_device(): jnp.stack([t_tile] * lax.axis_size('blk'))  14.3 us
  transfers between devices with their start and end apart: 2, of which 2 were waited for; matrix products, arithmetic and copies ran while one was open for 3% of the time, Pallas kernels for 0%

profile of v1, /device:TPU:6, one launch (start us, length us, event | category | flops | bytes accessed | tf_op | source)
XLA Modules:
  0.0 556.5 jit_solution(12032399735614322257)
XLA Ops:
  0.0 3.4 copy.17
  3.4 10.9 %stack.3 = f32[8,128,6400]{2,1,0:T(8,128)} broadcast(f32[128,6400]{1,0:T(8,128)S(1)} %copy.17), dimensions={1,2} | broadcast | bytes 29491200 | tf_op jit(solution)/shard_map/stack | solution.py:40
  14.3 6.9 %all-to-all-start = ((f32[8,128,6400]{2,1,0:T(8,128)}), f32[8,128,6400]{2,1,0:T(8,128)}, u32[]{:S(2)}, u32[]{:S(2)}) async-start(f32[8,128,6400]{2,1,0:T(8,128)} %stack.3), calls=%async_computation | async-start | bytes 52428800 | tf_op jit(solution)/shard_map/all_to_all | solution.py:40
  21.2 0.1 select_reduce_fusion.3
  21.3 0.1 copy.16
  21.5 0.1 reduce.1
  21.6 0.1 copy.15
  21.7 0.1 reduce
  21.9 0.1 reshape.233
  22.0 0.1 select_reduce_fusion.2
  22.1 0.2 select_reduce_fusion.1
  22.3 0.1 select_reduce_fusion
  22.4 2.6 scatter_custom_fusion
  25.0 9.5 %gather_fusion = s32[1536]{0:T(1024)S(1)} fusion(s32[512]{0:T(512)S(1)} %scatter_custom_fusion, s32[2048]{0:T(1024)S(1)} %pad_clamp_fusion.1), kind=kCustom, calls=%fused_computation | custom fusion | bytes 18432 | tf_op jit(solution)/shard_map/gather | solution.py:28
  34.6 0.1 iota_compare_fusion.4
  34.7 378.2 %all-to-all-done = f32[8,128,6400]{2,1,0:T(8,128)} async-done(((f32[8,128,6400]{2,1,0:T(8,128)}), f32[8,128,6400]{2,1,0:T(8,128)}, u32[]{:S(2)}, u32[]{:S(2)}) %all-to-all-start) | async-done | bytes 26214432 | tf_op jit(solution)/shard_map/all_to_all | solution.py:40
  412.9 45.8 %fusion.7 = f32[1024,512]{0,1:T(8,128)S(1)} fusion(f32[1024,6400]{1,0:T(8,128)} %bitcast.6, f32[6400,512]{1,0:T(8,128)} %bitcast.32), kind=kOutput, calls=%fused_computation.36 | convolution fusion | flops 40265318400 | bytes 41418752 | tf_op jit(solution)/shard_map/dot_general | solution.py:38
  458.8 5.8 %gather_fusion.1 = f32[1536,1024]{1,0:T(8,128)} fusion(f32[1024,512]{0,1:T(8,128)S(1)} %fusion.7, s32[2048]{0:T(1024)S(1)} %pad_clamp_fusion), kind=kCustom, calls=%fused_computation.1 | custom fusion | bytes 12589056 | tf_op jit(solution)/shard_map/jit(_take)/gather | solution.py:50
  464.6 4.9 select_select_fusion
  469.6 8.3 %all-to-all-start.1 = ((f32[1024,16,96]{0,2,1:T(8,128)}), f32[1024,16,96]{0,2,1:T(8,128)}, u32[]{:S(2)}, u32[]{:S(2)}) async-start(f32[1024,16,96]{0,2,1:T(8,128)} %select_select_fusion), calls=%async_computation.1 | async-start | bytes 12582912 | tf_op jit(solution)/shard_map/all_to_all | solution.py:52
  477.9 1.3 gather_fusion.2
  479.3 73.0 %all-to-all-done.1 = f32[1024,16,96]{0,2,1:T(8,128)} async-done(((f32[1024,16,96]{0,2,1:T(8,128)}), f32[1024,16,96]{0,2,1:T(8,128)}, u32[]{:S(2)}, u32[]{:S(2)}) %all-to-all-start.1) | async-done | bytes 6291488 | tf_op jit(solution)/shard_map/all_to_all | solution.py:52
  552.2 3.4 reduce_sum.52
  555.6 0.9 divide_select_fusion
  (23 shorter events, 0.4 us)
Async XLA Ops:
  0.0 477.9 %copy-start = (f32[512]{0:T(512)S(1)}, f32[512]{0:T(512)}, u32[]{:S(2)}) copy-start(f32[512]{0:T(512)} %param.8) | copy-start | bytes 6148
  14.3 6.9 %copy-start.1 = (s32[32]{0:T(128)S(1)}, s32[32]{0:T(128)}, u32[]{:S(2)}) copy-start(s32[32]{0:T(128)} %param.10) | copy-start | bytes 388
  14.3 6.9 %copy-start.3 = (s32[32]{0:T(128)S(1)}, s32[32]{0:T(128)}, u32[]{:S(2)}) copy-start(s32[32]{0:T(128)} %param.11) | copy-start | bytes 388
  14.3 398.6 %all-to-all-start = ((f32[8,128,6400]{2,1,0:T(8,128)}), f32[8,128,6400]{2,1,0:T(8,128)}, u32[]{:S(2)}, u32[]{:S(2)}) async-start(f32[8,128,6400]{2,1,0:T(8,128)} %stack.3), calls=%async_computation | async-start | bytes 52428800 | tf_op jit(solution)/shard_map/all_to_all | solution.py:40
  469.6 82.7 %all-to-all-start.1 = ((f32[1024,16,96]{0,2,1:T(8,128)}), f32[1024,16,96]{0,2,1:T(8,128)}, u32[]{:S(2)}, u32[]{:S(2)}) async-start(f32[1024,16,96]{0,2,1:T(8,128)} %select_select_fusion), calls=%async_computation.1 | async-start | bytes 12582912 | tf_op jit(solution)/shard_map/all_to_all | solution.py:52
  477.9 77.7 %copy-start.2 = (f32[1024]{0:T(1024)S(1)}, f32[1024]{0:T(1024)}, u32[]{:S(2)}) copy-start(f32[1024]{0:T(1024)} %param.9) | copy-start | bytes 12292
